TPU v7x, 512 devices: a whole 4x4x16 slice. The times are simulated.
512 devices in a mesh: group: 64 (over y, z), ingroup: 8 (over x, core).
Axes of the slice: x: 4, y: 4, z: 16, core: 2. Of those that a mesh axis runs over, the one named last changes fastest.
Arguments:
- multipoles: bfloat16 [338, 65536], P(None, ('group', 'ingroup')), may hold values from -6 to 6
- interaction_lists: int32 [6, 36, 65536], P(None, None, ('group', 'ingroup')), may hold values from -1 to 671, as said below
- ghost_exports: int32 [512, 512], P(('group', 'ingroup')), may hold values from 0 to 127, as said below
- sibling_exports: int32 [512, 4], P(('group', 'ingroup')), may hold values from 0 to 127, as said below
- box_counts: int32 [512], P(('group', 'ingroup')), may hold values from 32 to 128, as said below
- multipole_to_plane: bfloat16 [1440, 338], replicated, may hold values from -0.3125 to 0.3125
- plane_shifts: float32 [6, 36, 240], replicated, may hold values from -1 to 1, as said below
- plane_to_local: bfloat16 [338, 1440], replicated, may hold values from -0.15625 to 0.15625
Outputs:
- local_expansions: bfloat16 [338, 65536], P(None, ('group', 'ingroup'))
Inputs may be any that keep to these rules, and one draw needn't show every extreme that they name: `interaction_lists`: columns below 128 are live box slots of the target's own device; the others index the sibling and slab parts of its source table. `ghost_exports`: every entry is a live box slot of the exporting device, below its count. `sibling_exports`: every entry is a live box slot of the exporting device, below its count. `box_counts`: some device has exactly 128 live boxes in every draw. `plane_shifts`: each complex factor has magnitude at most 1.
All inputs are finite; a program needn't handle non-finite values.
Results may differ from a plain program's by a relative error of at most 0.0058.
Values may be sent and summed in bfloat16 or wider, within the bound.
A program may use at most 64 MiB of HBM per device.

v0:
```python
import jax
import jax.numpy as jnp
from jax import lax
from jax.sharding import PartitionSpec as P


def expand(multipole_to_plane, columns):
    return jnp.dot(multipole_to_plane, columns, preferred_element_type=jnp.float32).astype(
        jnp.bfloat16
    )


def exponential(box_table, slot_lists, plane_shifts):
    directions = plane_shifts.shape[0]
    list_slots = plane_shifts.shape[1]
    width = plane_shifts.shape[2]
    nodes = width // 2
    block = slot_lists.shape[2]
    table = box_table.reshape(directions, width, box_table.shape[1])

    def add_slot(sums, slot):
        real_sum, imaginary_sum = sums
        index = lax.dynamic_index_in_dim(slot_lists, slot, 1, False)
        safe_index = jnp.maximum(index, 0)[:, None, :]
        picked = jnp.take_along_axis(table, safe_index, axis=2).astype(jnp.float32)
        picked = jnp.where((index >= 0)[:, None, :], picked, jnp.float32(0.0))
        factors = lax.dynamic_index_in_dim(plane_shifts, slot, 1, False)
        real_factor = factors[:, :nodes][:, :, None]
        imaginary_factor = factors[:, nodes:][:, :, None]
        real_part = picked[:, :nodes]
        imaginary_part = picked[:, nodes:]
        real_sum = real_sum + real_factor * real_part - imaginary_factor * imaginary_part
        imaginary_sum = imaginary_sum + real_factor * imaginary_part + imaginary_factor * real_part
        return (real_sum, imaginary_sum)

    def four_slots(turn, sums):
        for offset in range(4):
            sums = add_slot(sums, turn * 4 + offset)
        return sums

    zeros = jnp.zeros((directions, nodes, block), jnp.float32)
    real_sum, imaginary_sum = lax.fori_loop(0, list_slots // 4, four_slots, (zeros, zeros))
    joined = jnp.concatenate([real_sum, imaginary_sum], axis=1)
    return joined.reshape(directions * width, block).astype(jnp.bfloat16)


def per_device(
    multipoles,
    interaction_lists,
    ghost_exports,
    sibling_exports,
    box_counts,
    multipole_to_plane,
    plane_shifts,
    plane_to_local,
):
    capacity = multipoles.shape[1]
    live_count = box_counts[0]
    sources = expand(multipole_to_plane, multipoles)
    sibling = lax.all_gather(
        jnp.take(sources, sibling_exports[0], axis=1), "ingroup", axis=1, tiled=True
    )
    remote = lax.all_to_all(
        jnp.take(sources, ghost_exports[0], axis=1),
        "group",
        split_axis=1,
        concat_axis=1,
        tiled=True,
    )
    box_table = jnp.concatenate([sources, sibling, remote], axis=1)
    block_width = min(128, capacity)

    def one_block(step, result):
        start = step * block_width
        exponentials = exponential(box_table, interaction_lists, plane_shifts)
        local_terms = jnp.dot(plane_to_local, exponentials, preferred_element_type=jnp.float32)
        live_mask = start + jnp.arange(block_width, dtype=jnp.int32) < live_count
        finished = jnp.where(live_mask[None], local_terms, jnp.float32(0.0)).astype(jnp.bfloat16)
        return finished

    block_limit = capacity // block_width
    initial = jnp.zeros((plane_to_local.shape[0], capacity), jnp.bfloat16)
    return lax.fori_loop(0, block_limit, one_block, initial)


def solution(mesh):
    return jax.shard_map(
        per_device,
        mesh=mesh,
        in_specs=(
            P(None, ("group", "ingroup")),
            P(None, None, ("group", "ingroup")),
            P(("group", "ingroup"), None),
            P(("group", "ingroup"), None),
            P(("group", "ingroup")),
            P(),
            P(),
            P(),
        ),
        out_specs=P(None, ("group", "ingroup")),
        check_vma=False,
    )
```

profile of v0, /device:TPU:8, one launch (start us, length us, event | category | flops | bytes accessed | tf_op | source)
XLA Modules:
  0.0 416.9 jit_solution(7160300579876677647)
XLA Ops:
  7.7 18.9 %all-to-all-start = ((bf16[1440,64,8]{0,2,1:T(8,128)(2,1)}), bf16[1440,64,8]{0,2,1:T(8,128)(2,1)S(1)}, u32[]{:S(2)}, u32[]{:S(2)}) async-start(bf16[1440,64,8]{0,2,1:T(8,128)(2,1)} %bitcast_select_fusion), calls=%async_computation | async-start | bytes 3145728 | tf_op jit(solution)/shard_map/all_to_all | solution.py:63
  27.3 13.2 %all-gather = bf16[8,4,1440]{2,1,0:T(4,128)(2,1)S(1)} all-gather(bf16[1,4,1440]{2,1,0:T(4,128)(2,1)S(1)} %select_bitcast_fusion), channel_id=1, replica_groups=mesh['group'=64,'ingroup'=8] {'ingroup'}, dimensions={0}, use_global_device_ids=true | all-gather | bytes 103680 | tf_op jit(solution)/shard_map/all_gather | solution.py:60
  45.1 57.6 %all-to-all-done = bf16[1440,64,8]{0,2,1:T(8,128)(2,1)S(1)} async-done(((bf16[1440,64,8]{0,2,1:T(8,128)(2,1)}), bf16[1440,64,8]{0,2,1:T(8,128)(2,1)S(1)}, u32[]{:S(2)}, u32[]{:S(2)}) %all-to-all-start) | async-done | bytes 1474592 | tf_op jit(solution)/shard_map/all_to_all | solution.py:63
  109.3 304.1 %while.27 = (s32[]{:T(128)}, f32[6,120,128]{1,2,0:T(8,128)}, f32[6,120,128]{1,2,0:T(8,128)}, f32[6,36,240]{2,0,1:T(8,128)}, s32[6,36,128]{2,0,1:T(8,128)}, /*ind...) while((s32[]{:T(128)}, f32[6,120,128]{1,2,0:T(8,128)}, ...), condition=%wide.region_1.3_spmd.clone, body=%wide.region_0.0_spmd.clone.sunk | while | flops 5368339 | bytes 29703716 | solution.py:42
  110.0 4.4 %gather_fusion.2 = bf16[768,240]{1,0:T(8,128)(2,1)S(1)} fusion(bf16[6,240,672]{1,2,0:T(8,128)(2,1)S(1)} %get-tuple-element.407, s32[768]{0:T(1024)S(1)} %get-tuple-element.352), kind=kCustom, calls=%fused_computation.1.clone.clone.1 | custom fusion | bytes 743424 | tf_op jit(solution)/shard_map/while/body/eval_jaxpr/while/body/eval_jaxpr/jit(take_along_axis)/gather | solution.py:25
  114.4 6.3 %gather_fusion.3 = bf16[768,240]{1,0:T(8,128)(2,1)} fusion(bf16[6,240,672]{1,2,0:T(8,128)(2,1)S(1)} %get-tuple-element.407, s32[768]{0:T(1024)S(1)} %get-tuple-element.355), kind=kCustom, calls=%fused_computation.clone.clone.1 | custom fusion | bytes 743424 | tf_op jit(solution)/shard_map/while/body/eval_jaxpr/while/body/eval_jaxpr/jit(take_along_axis)/gather | solution.py:25
  123.9 4.4 %gather_fusion = bf16[768,240]{1,0:T(8,128)(2,1)S(1)} fusion(bf16[6,240,672]{1,2,0:T(8,128)(2,1)S(1)} %get-tuple-element.407, s32[768]{0:T(1024)S(1)} %get-tuple-element.344), kind=kCustom, calls=%fused_computation.3.clone.clone.1 | custom fusion | bytes 743424 | tf_op jit(solution)/shard_map/while/body/eval_jaxpr/while/body/eval_jaxpr/jit(take_along_axis)/gather | solution.py:25
  128.3 6.3 %gather_fusion.1 = bf16[768,240]{1,0:T(8,128)(2,1)} fusion(bf16[6,240,672]{1,2,0:T(8,128)(2,1)S(1)} %get-tuple-element.407, s32[768]{0:T(1024)S(1)} %get-tuple-element.347), kind=kCustom, calls=%fused_computation.2.clone.clone.1 | custom fusion | bytes 743424 | tf_op jit(solution)/shard_map/while/body/eval_jaxpr/while/body/eval_jaxpr/jit(take_along_axis)/gather | solution.py:25
  143.7 4.4 %gather_fusion.2 = bf16[768,240]{1,0:T(8,128)(2,1)S(1)} fusion(bf16[6,240,672]{1,2,0:T(8,128)(2,1)S(1)} %get-tuple-element.407, s32[768]{0:T(1024)S(1)} %get-tuple-element.352), kind=kCustom, calls=%fused_computation.1.clone.clone.1 | custom fusion | bytes 743424 | tf_op jit(solution)/shard_map/while/body/eval_jaxpr/while/body/eval_jaxpr/jit(take_along_axis)/gather | solution.py:25
  148.1 6.3 %gather_fusion.3 = bf16[768,240]{1,0:T(8,128)(2,1)} fusion(bf16[6,240,672]{1,2,0:T(8,128)(2,1)S(1)} %get-tuple-element.407, s32[768]{0:T(1024)S(1)} %get-tuple-element.355), kind=kCustom, calls=%fused_computation.clone.clone.1 | custom fusion | bytes 743424 | tf_op jit(solution)/shard_map/while/body/eval_jaxpr/while/body/eval_jaxpr/jit(take_along_axis)/gather | solution.py:25
  157.5 4.4 %gather_fusion = bf16[768,240]{1,0:T(8,128)(2,1)S(1)} fusion(bf16[6,240,672]{1,2,0:T(8,128)(2,1)S(1)} %get-tuple-element.407, s32[768]{0:T(1024)S(1)} %get-tuple-element.344), kind=kCustom, calls=%fused_computation.3.clone.clone.1 | custom fusion | bytes 743424 | tf_op jit(solution)/shard_map/while/body/eval_jaxpr/while/body/eval_jaxpr/jit(take_along_axis)/gather | solution.py:25
  161.9 6.3 %gather_fusion.1 = bf16[768,240]{1,0:T(8,128)(2,1)} fusion(bf16[6,240,672]{1,2,0:T(8,128)(2,1)S(1)} %get-tuple-element.407, s32[768]{0:T(1024)S(1)} %get-tuple-element.347), kind=kCustom, calls=%fused_computation.2.clone.clone.1 | custom fusion | bytes 743424 | tf_op jit(solution)/shard_map/while/body/eval_jaxpr/while/body/eval_jaxpr/jit(take_along_axis)/gather | solution.py:25
  171.6 3.9 fusion.38
  177.5 4.4 %gather_fusion.2 = bf16[768,240]{1,0:T(8,128)(2,1)S(1)} fusion(bf16[6,240,672]{1,2,0:T(8,128)(2,1)S(1)} %get-tuple-element.407, s32[768]{0:T(1024)S(1)} %get-tuple-element.352), kind=kCustom, calls=%fused_computation.1.clone.clone.1 | custom fusion | bytes 743424 | tf_op jit(solution)/shard_map/while/body/eval_jaxpr/while/body/eval_jaxpr/jit(take_along_axis)/gather | solution.py:25
  181.9 6.3 %gather_fusion.3 = bf16[768,240]{1,0:T(8,128)(2,1)} fusion(bf16[6,240,672]{1,2,0:T(8,128)(2,1)S(1)} %get-tuple-element.407, s32[768]{0:T(1024)S(1)} %get-tuple-element.355), kind=kCustom, calls=%fused_computation.clone.clone.1 | custom fusion | bytes 743424 | tf_op jit(solution)/shard_map/while/body/eval_jaxpr/while/body/eval_jaxpr/jit(take_along_axis)/gather | solution.py:25
  191.3 4.4 %gather_fusion = bf16[768,240]{1,0:T(8,128)(2,1)S(1)} fusion(bf16[6,240,672]{1,2,0:T(8,128)(2,1)S(1)} %get-tuple-element.407, s32[768]{0:T(1024)S(1)} %get-tuple-element.344), kind=kCustom, calls=%fused_computation.3.clone.clone.1 | custom fusion | bytes 743424 | tf_op jit(solution)/shard_map/while/body/eval_jaxpr/while/body/eval_jaxpr/jit(take_along_axis)/gather | solution.py:25
  195.7 6.3 %gather_fusion.1 = bf16[768,240]{1,0:T(8,128)(2,1)} fusion(bf16[6,240,672]{1,2,0:T(8,128)(2,1)S(1)} %get-tuple-element.407, s32[768]{0:T(1024)S(1)} %get-tuple-element.347), kind=kCustom, calls=%fused_computation.2.clone.clone.1 | custom fusion | bytes 743424 | tf_op jit(solution)/shard_map/while/body/eval_jaxpr/while/body/eval_jaxpr/jit(take_along_axis)/gather | solution.py:25
  205.4 3.9 fusion.38
  211.3 4.4 %gather_fusion.2 = bf16[768,240]{1,0:T(8,128)(2,1)S(1)} fusion(bf16[6,240,672]{1,2,0:T(8,128)(2,1)S(1)} %get-tuple-element.407, s32[768]{0:T(1024)S(1)} %get-tuple-element.352), kind=kCustom, calls=%fused_computation.1.clone.clone.1 | custom fusion | bytes 743424 | tf_op jit(solution)/shard_map/while/body/eval_jaxpr/while/body/eval_jaxpr/jit(take_along_axis)/gather | solution.py:25
  215.7 6.3 %gather_fusion.3 = bf16[768,240]{1,0:T(8,128)(2,1)} fusion(bf16[6,240,672]{1,2,0:T(8,128)(2,1)S(1)} %get-tuple-element.407, s32[768]{0:T(1024)S(1)} %get-tuple-element.355), kind=kCustom, calls=%fused_computation.clone.clone.1 | custom fusion | bytes 743424 | tf_op jit(solution)/shard_map/while/body/eval_jaxpr/while/body/eval_jaxpr/jit(take_along_axis)/gather | solution.py:25
  225.1 4.4 %gather_fusion = bf16[768,240]{1,0:T(8,128)(2,1)S(1)} fusion(bf16[6,240,672]{1,2,0:T(8,128)(2,1)S(1)} %get-tuple-element.407, s32[768]{0:T(1024)S(1)} %get-tuple-element.344), kind=kCustom, calls=%fused_computation.3.clone.clone.1 | custom fusion | bytes 743424 | tf_op jit(solution)/shard_map/while/body/eval_jaxpr/while/body/eval_jaxpr/jit(take_along_axis)/gather | solution.py:25
  229.5 6.3 %gather_fusion.1 = bf16[768,240]{1,0:T(8,128)(2,1)} fusion(bf16[6,240,672]{1,2,0:T(8,128)(2,1)S(1)} %get-tuple-element.407, s32[768]{0:T(1024)S(1)} %get-tuple-element.347), kind=kCustom, calls=%fused_computation.2.clone.clone.1 | custom fusion | bytes 743424 | tf_op jit(solution)/shard_map/while/body/eval_jaxpr/while/body/eval_jaxpr/jit(take_along_axis)/gather | solution.py:25
  239.2 3.9 fusion.38
  245.1 4.4 %gather_fusion.2 = bf16[768,240]{1,0:T(8,128)(2,1)S(1)} fusion(bf16[6,240,672]{1,2,0:T(8,128)(2,1)S(1)} %get-tuple-element.407, s32[768]{0:T(1024)S(1)} %get-tuple-element.352), kind=kCustom, calls=%fused_computation.1.clone.clone.1 | custom fusion | bytes 743424 | tf_op jit(solution)/shard_map/while/body/eval_jaxpr/while/body/eval_jaxpr/jit(take_along_axis)/gather | solution.py:25
  249.5 6.3 %gather_fusion.3 = bf16[768,240]{1,0:T(8,128)(2,1)} fusion(bf16[6,240,672]{1,2,0:T(8,128)(2,1)S(1)} %get-tuple-element.407, s32[768]{0:T(1024)S(1)} %get-tuple-element.355), kind=kCustom, calls=%fused_computation.clone.clone.1 | custom fusion | bytes 743424 | tf_op jit(solution)/shard_map/while/body/eval_jaxpr/while/body/eval_jaxpr/jit(take_along_axis)/gather | solution.py:25
  258.9 4.4 %gather_fusion = bf16[768,240]{1,0:T(8,128)(2,1)S(1)} fusion(bf16[6,240,672]{1,2,0:T(8,128)(2,1)S(1)} %get-tuple-element.407, s32[768]{0:T(1024)S(1)} %get-tuple-element.344), kind=kCustom, calls=%fused_computation.3.clone.clone.1 | custom fusion | bytes 743424 | tf_op jit(solution)/shard_map/while/body/eval_jaxpr/while/body/eval_jaxpr/jit(take_along_axis)/gather | solution.py:25
  263.3 6.3 %gather_fusion.1 = bf16[768,240]{1,0:T(8,128)(2,1)} fusion(bf16[6,240,672]{1,2,0:T(8,128)(2,1)S(1)} %get-tuple-element.407, s32[768]{0:T(1024)S(1)} %get-tuple-element.347), kind=kCustom, calls=%fused_computation.2.clone.clone.1 | custom fusion | bytes 743424 | tf_op jit(solution)/shard_map/while/body/eval_jaxpr/while/body/eval_jaxpr/jit(take_along_axis)/gather | solution.py:25
  272.9 3.9 fusion.38
  278.9 4.4 %gather_fusion.2 = bf16[768,240]{1,0:T(8,128)(2,1)S(1)} fusion(bf16[6,240,672]{1,2,0:T(8,128)(2,1)S(1)} %get-tuple-element.407, s32[768]{0:T(1024)S(1)} %get-tuple-element.352), kind=kCustom, calls=%fused_computation.1.clone.clone.1 | custom fusion | bytes 743424 | tf_op jit(solution)/shard_map/while/body/eval_jaxpr/while/body/eval_jaxpr/jit(take_along_axis)/gather | solution.py:25
  283.3 6.3 %gather_fusion.3 = bf16[768,240]{1,0:T(8,128)(2,1)} fusion(bf16[6,240,672]{1,2,0:T(8,128)(2,1)S(1)} %get-tuple-element.407, s32[768]{0:T(1024)S(1)} %get-tuple-element.355), kind=kCustom, calls=%fused_computation.clone.clone.1 | custom fusion | bytes 743424 | tf_op jit(solution)/shard_map/while/body/eval_jaxpr/while/body/eval_jaxpr/jit(take_along_axis)/gather | solution.py:25
  292.7 4.4 %gather_fusion = bf16[768,240]{1,0:T(8,128)(2,1)S(1)} fusion(bf16[6,240,672]{1,2,0:T(8,128)(2,1)S(1)} %get-tuple-element.407, s32[768]{0:T(1024)S(1)} %get-tuple-element.344), kind=kCustom, calls=%fused_computation.3.clone.clone.1 | custom fusion | bytes 743424 | tf_op jit(solution)/shard_map/while/body/eval_jaxpr/while/body/eval_jaxpr/jit(take_along_axis)/gather | solution.py:25
  297.1 6.3 %gather_fusion.1 = bf16[768,240]{1,0:T(8,128)(2,1)} fusion(bf16[6,240,672]{1,2,0:T(8,128)(2,1)S(1)} %get-tuple-element.407, s32[768]{0:T(1024)S(1)} %get-tuple-element.347), kind=kCustom, calls=%fused_computation.2.clone.clone.1 | custom fusion | bytes 743424 | tf_op jit(solution)/shard_map/while/body/eval_jaxpr/while/body/eval_jaxpr/jit(take_along_axis)/gather | solution.py:25
  306.7 3.9 fusion.38
  312.7 4.4 %gather_fusion.2 = bf16[768,240]{1,0:T(8,128)(2,1)S(1)} fusion(bf16[6,240,672]{1,2,0:T(8,128)(2,1)S(1)} %get-tuple-element.407, s32[768]{0:T(1024)S(1)} %get-tuple-element.352), kind=kCustom, calls=%fused_computation.1.clone.clone.1 | custom fusion | bytes 743424 | tf_op jit(solution)/shard_map/while/body/eval_jaxpr/while/body/eval_jaxpr/jit(take_along_axis)/gather | solution.py:25
  317.1 6.3 %gather_fusion.3 = bf16[768,240]{1,0:T(8,128)(2,1)} fusion(bf16[6,240,672]{1,2,0:T(8,128)(2,1)S(1)} %get-tuple-element.407, s32[768]{0:T(1024)S(1)} %get-tuple-element.355), kind=kCustom, calls=%fused_computation.clone.clone.1 | custom fusion | bytes 743424 | tf_op jit(solution)/shard_map/while/body/eval_jaxpr/while/body/eval_jaxpr/jit(take_along_axis)/gather | solution.py:25
  326.5 4.4 %gather_fusion = bf16[768,240]{1,0:T(8,128)(2,1)S(1)} fusion(bf16[6,240,672]{1,2,0:T(8,128)(2,1)S(1)} %get-tuple-element.407, s32[768]{0:T(1024)S(1)} %get-tuple-element.344), kind=kCustom, calls=%fused_computation.3.clone.clone.1 | custom fusion | bytes 743424 | tf_op jit(solution)/shard_map/while/body/eval_jaxpr/while/body/eval_jaxpr/jit(take_along_axis)/gather | solution.py:25
  330.9 6.3 %gather_fusion.1 = bf16[768,240]{1,0:T(8,128)(2,1)} fusion(bf16[6,240,672]{1,2,0:T(8,128)(2,1)S(1)} %get-tuple-element.407, s32[768]{0:T(1024)S(1)} %get-tuple-element.347), kind=kCustom, calls=%fused_computation.2.clone.clone.1 | custom fusion | bytes 743424 | tf_op jit(solution)/shard_map/while/body/eval_jaxpr/while/body/eval_jaxpr/jit(take_along_axis)/gather | solution.py:25
  340.5 3.9 fusion.38
  346.5 4.4 %gather_fusion.2 = bf16[768,240]{1,0:T(8,128)(2,1)S(1)} fusion(bf16[6,240,672]{1,2,0:T(8,128)(2,1)S(1)} %get-tuple-element.407, s32[768]{0:T(1024)S(1)} %get-tuple-element.352), kind=kCustom, calls=%fused_computation.1.clone.clone.1 | custom fusion | bytes 743424 | tf_op jit(solution)/shard_map/while/body/eval_jaxpr/while/body/eval_jaxpr/jit(take_along_axis)/gather | solution.py:25
  350.9 6.3 %gather_fusion.3 = bf16[768,240]{1,0:T(8,128)(2,1)} fusion(bf16[6,240,672]{1,2,0:T(8,128)(2,1)S(1)} %get-tuple-element.407, s32[768]{0:T(1024)S(1)} %get-tuple-element.355), kind=kCustom, calls=%fused_computation.clone.clone.1 | custom fusion | bytes 743424 | tf_op jit(solution)/shard_map/while/body/eval_jaxpr/while/body/eval_jaxpr/jit(take_along_axis)/gather | solution.py:25
  360.3 4.4 %gather_fusion = bf16[768,240]{1,0:T(8,128)(2,1)S(1)} fusion(bf16[6,240,672]{1,2,0:T(8,128)(2,1)S(1)} %get-tuple-element.407, s32[768]{0:T(1024)S(1)} %get-tuple-element.344), kind=kCustom, calls=%fused_computation.3.clone.clone.1 | custom fusion | bytes 743424 | tf_op jit(solution)/shard_map/while/body/eval_jaxpr/while/body/eval_jaxpr/jit(take_along_axis)/gather | solution.py:25
  364.7 6.3 %gather_fusion.1 = bf16[768,240]{1,0:T(8,128)(2,1)} fusion(bf16[6,240,672]{1,2,0:T(8,128)(2,1)S(1)} %get-tuple-element.407, s32[768]{0:T(1024)S(1)} %get-tuple-element.347), kind=kCustom, calls=%fused_computation.2.clone.clone.1 | custom fusion | bytes 743424 | tf_op jit(solution)/shard_map/while/body/eval_jaxpr/while/body/eval_jaxpr/jit(take_along_axis)/gather | solution.py:25
  374.3 3.9 fusion.38
  380.2 4.4 %gather_fusion.2 = bf16[768,240]{1,0:T(8,128)(2,1)S(1)} fusion(bf16[6,240,672]{1,2,0:T(8,128)(2,1)S(1)} %get-tuple-element.407, s32[768]{0:T(1024)S(1)} %get-tuple-element.352), kind=kCustom, calls=%fused_computation.1.clone.clone.1 | custom fusion | bytes 743424 | tf_op jit(solution)/shard_map/while/body/eval_jaxpr/while/body/eval_jaxpr/jit(take_along_axis)/gather | solution.py:25
  384.7 6.3 %gather_fusion.3 = bf16[768,240]{1,0:T(8,128)(2,1)} fusion(bf16[6,240,672]{1,2,0:T(8,128)(2,1)S(1)} %get-tuple-element.407, s32[768]{0:T(1024)S(1)} %get-tuple-element.355), kind=kCustom, calls=%fused_computation.clone.clone.1 | custom fusion | bytes 743424 | tf_op jit(solution)/shard_map/while/body/eval_jaxpr/while/body/eval_jaxpr/jit(take_along_axis)/gather | solution.py:25
  394.1 4.4 %gather_fusion = bf16[768,240]{1,0:T(8,128)(2,1)S(1)} fusion(bf16[6,240,672]{1,2,0:T(8,128)(2,1)S(1)} %get-tuple-element.407, s32[768]{0:T(1024)S(1)} %get-tuple-element.344), kind=kCustom, calls=%fused_computation.3.clone.clone.1 | custom fusion | bytes 743424 | tf_op jit(solution)/shard_map/while/body/eval_jaxpr/while/body/eval_jaxpr/jit(take_along_axis)/gather | solution.py:25
  398.5 6.3 %gather_fusion.1 = bf16[768,240]{1,0:T(8,128)(2,1)} fusion(bf16[6,240,672]{1,2,0:T(8,128)(2,1)S(1)} %get-tuple-element.407, s32[768]{0:T(1024)S(1)} %get-tuple-element.347), kind=kCustom, calls=%fused_computation.2.clone.clone.1 | custom fusion | bytes 743424 | tf_op jit(solution)/shard_map/while/body/eval_jaxpr/while/body/eval_jaxpr/jit(take_along_axis)/gather | solution.py:25
  408.1 3.9 fusion.38
  (221 shorter events, 102.1 us)
Async XLA Ops:
  7.7 18.9 %copy-start.10 = (s32[1,4]{1,0:T(1,128)S(1)}, s32[1,4]{1,0:T(1,128)}, u32[]{:S(2)}) copy-start(s32[1,4]{1,0:T(1,128)} %param.15) | copy-start | bytes 52
  7.7 95.0 %all-to-all-start = ((bf16[1440,64,8]{0,2,1:T(8,128)(2,1)}), bf16[1440,64,8]{0,2,1:T(8,128)(2,1)S(1)}, u32[]{:S(2)}, u32[]{:S(2)}) async-start(bf16[1440,64,8]{0,2,1:T(8,128)(2,1)} %bitcast_select_fusion), calls=%async_computation | async-start | bytes 3145728 | tf_op jit(solution)/shard_map/all_to_all | solution.py:63
  27.2 16.5 %copy-start.8 = (s32[6,36,128]{2,1,0:T(8,128)S(1)}, s32[6,36,128]{2,1,0:T(8,128)}, u32[]{:S(2)}) copy-start(s32[6,36,128]{2,1,0:T(8,128)} %param.13) | copy-start | bytes 331780
  137.9 3.8 copy-start.1
  137.9 3.8 copy-start.2
  137.9 3.8 copy-start.3
  137.9 3.8 copy-start.4
  137.9 3.8 copy-start.5
  171.5 3.9 copy-start.1
  171.5 3.9 copy-start.2
  171.6 3.9 copy-start.3
  171.6 3.9 copy-start.4
  171.6 3.9 copy-start.5
  205.3 3.9 copy-start.1
  205.3 3.9 copy-start.2
  205.3 3.9 copy-start.3
  205.3 3.9 copy-start.4
  205.3 3.9 copy-start.5
  239.1 3.9 copy-start.1
  239.1 3.9 copy-start.2
  239.1 3.9 copy-start.3
  239.1 3.9 copy-start.4
  239.1 3.9 copy-start.5
  272.9 3.9 copy-start.1
  272.9 3.9 copy-start.2
  272.9 3.9 copy-start.3
  272.9 3.9 copy-start.4
  272.9 3.9 copy-start.5
  306.7 3.9 copy-start.1
  306.7 3.9 copy-start.2
  306.7 3.9 copy-start.3
  306.7 3.9 copy-start.4
  306.7 3.9 copy-start.5
  340.5 3.9 copy-start.1
  340.5 3.9 copy-start.2
  340.5 3.9 copy-start.3
  340.5 3.9 copy-start.4
  340.5 3.9 copy-start.5
  374.3 3.9 copy-start.1
  374.3 3.9 copy-start.2
  374.3 3.9 copy-start.3
  374.3 3.9 copy-start.4
  374.3 3.9 copy-start.5
  408.1 3.9 copy-start.1
  408.1 3.9 copy-start.2
  408.1 3.9 copy-start.3
  408.1 3.9 copy-start.4
  408.1 3.9 copy-start.5
  (12 other events, 13.5 us)
where the time goes:
time: 419 us; the launch traced here: 417 us
  local copies, waits for them, and re-layouts  223 us (53%)
  other arithmetic  100 us (24%)
  waiting for transfers between devices  57.6 us (14%)
  starting transfers between devices  18.9 us (5%)
  blocking collectives  13.2 us (3%)
    gather x36, local copies, waits for them, and re-layouts, add_slot(): picked = jnp.take_along_axis(table, safe_index, axis=2).astype(jnp.float32)  193 us
    all_to_all x1, waiting for transfers between devices, per_device(): lax.all_to_all(jnp.take(sources, ghost_exports[0], axis=1), 'group', spli...  57.6 us
    select_n x18, other arithmetic, add_slot(): picked = jnp.where((index >= 0)[:, None, :], picked, jnp.float32(0.0))  43.5 us
    add x9, other arithmetic, add_slot(): imaginary_sum + real_factor * imaginary_part + imaginary_factor * real_part  34.6 us
    all_to_all x1, starting transfers between devices, per_device(): lax.all_to_all(jnp.take(sources, ghost_exports[0], axis=1), 'group', spli...  18.9 us
    all_gather x1, blocking collectives, per_device(): lax.all_gather(jnp.take(sources, sibling_exports[0], axis=1), 'ingroup',...  13.2 us
  transfers between devices with their start and end apart: 1, of which 1 were waited for; matrix products, arithmetic and copies ran while one was open for 1% of the time, Pallas kernels for 0%

commit v1 on v0

v1 whole, which is shorter than its diff:
```python
import functools

import jax
import jax.numpy as jnp
from jax import lax
from jax.experimental import pallas as pl
from jax.experimental.pallas import tpu as pltpu
from jax.sharding import PartitionSpec as P

MESH = pl.DeviceIdType.MESH
BF16, F32, I32 = jnp.bfloat16, jnp.float32, jnp.int32

LANES = 128
TILE = 256
NY, NZ = 4, 16
NSIB = 8
STACK = 4
WIDE = 384
SERVE = ((6, 7), (0, 3), (3, 3))


def columns_of(row, count):
    wide = jnp.broadcast_to(row.astype(F32), (LANES, count))
    return jnp.concatenate([wide[:, c : c + LANES].T for c in range(0, count, LANES)], axis=0)


def kernel(
    mult_ref, lists_ref, ghost_ref, sibx_ref, count_ref, m2p_ref, shifts_ref, p2l_ref, out_ref,
    mult_pad, m2p_pad, p2l_pad, shift_pad, rel, send, sib_send, own_x, sib_recv, recv, planes, acc,
    send_sem, sib_send_sem, sib_sem, tile_sem, in1_sem, in2_sem, go1_sem, go2_sem,
):
    g = lax.axis_index("group")
    i = lax.axis_index("ingroup")
    y, z = g // NZ, lax.rem(g, NZ)
    first, second, third = z < 4, (z >= 4) & (z < 8), z >= 8
    low = z < 8
    dirs, slots = lists_ref.shape[0], lists_ref.shape[1]
    mreal, cap = mult_ref.shape
    nodes = shifts_ref.shape[2] // 2

    def signal(sem, slab):
        pl.semaphore_signal(sem, 1, device_id=(slab, i), device_id_type=MESH)

    barrier = pltpu.get_barrier_semaphore()

    def greet_sibling(n, c):
        pl.semaphore_signal(barrier, 1, device_id=(g, lax.rem(i + n, NSIB)), device_id_type=MESH)
        return c

    lax.fori_loop(1, NSIB, greet_sibling, 0)

    @pl.when(first)
    def _():
        def greet(n, c):
            signal(barrier, lax.rem(g + n, NY * NZ))
            return c

        lax.fori_loop(1, NY * NZ, greet, 0)

    mult_pad[...] = jnp.zeros_like(mult_pad)
    mult_pad[:mreal, :] = mult_ref[...]
    lane = lax.broadcasted_iota(I32, (LANES, LANES), 1).astype(F32)

    def pick(cols):
        lanes = lax.broadcasted_iota(I32, cols.shape, 1).astype(F32)
        hot = jnp.where(cols == lanes, F32(1), F32(0)).astype(BF16)
        rows = lax.dot_general(hot, mult_pad[...], (((1,), (1,)), ((), ())), preferred_element_type=F32)
        return rows.astype(BF16)

    n_ghost = ghost_ref.shape[1]
    send[...] = pick(columns_of(ghost_ref[...], n_ghost)).reshape(send.shape)
    sib_row = jnp.concatenate([sibx_ref[...], jnp.full((1, LANES - sibx_ref.shape[1]), -1, I32)], axis=1)
    sib_send[...] = pick(columns_of(sib_row, LANES)[: sib_send.shape[0]])
    sib_recv[i] = sib_send[...]

    @pl.when(low)
    def _():
        recv[0, y * 8 + lax.rem(z, 8)] = send[g]

    @pl.when(third)
    def _():
        recv[1, y * 8 + lax.rem(z, 8)] = send[g]

    @pl.when(first)
    def _():
        pl.semaphore_wait(barrier, 7 + 15)

    @pl.when(jnp.logical_not(first))
    def _():
        pl.semaphore_wait(barrier, 7 + 16)

    def report(sem):
        def one(n, c):
            signal(sem, lax.rem(y + n // 4, NY) * NZ + lax.rem(n, 4))
            return c

        lax.fori_loop(0, 16, one, 0)

    @pl.when(second)
    def _():
        report(in1_sem)

    @pl.when(third)
    def _():
        report(in2_sem)

    side = z // 8
    slot = y * 8 + lax.rem(z, 8)

    def send_to(slab):
        @pl.when(slab != g)
        def _():
            pltpu.make_async_remote_copy(
                src_ref=send.at[slab],
                dst_ref=recv.at[side, slot],
                send_sem=send_sem,
                recv_sem=tile_sem.at[side],
                device_id=(slab, i),
                device_id_type=MESH,
            ).start()

    def send_sib(n, c):
        pltpu.make_async_remote_copy(
            src_ref=sib_send,
            dst_ref=sib_recv.at[i],
            send_sem=sib_send_sem,
            recv_sem=sib_sem,
            device_id=(g, lax.rem(i + n, NSIB)),
            device_id_type=MESH,
        ).start()
        return c

    lax.fori_loop(1, NSIB, send_sib, 0)

    def serve(base, width):
        def one(n, c):
            zz = n // NY
            if width == 8:
                zz = lax.rem(zz + z, 8)
            send_to(lax.rem(y + n, NY) * NZ + base + zz)
            return c

        lax.fori_loop(0, NY * width, one, 0)

    serve(0, 4)

    own_x[...] = jnp.zeros_like(own_x)
    own_x[:cap] = pick(lax.broadcasted_iota(I32, (LANES, LANES), 0).astype(F32))
    m2p_pad[...] = jnp.zeros_like(m2p_pad)
    p2l_pad[...] = jnp.zeros_like(p2l_pad)
    shift_pad[...] = jnp.zeros_like(shift_pad)
    acc[...] = jnp.zeros_like(acc)
    for d in range(dirs):
        for h in range(2):
            at = (2 * d + h) * nodes
            m2p_pad[d, h * LANES : h * LANES + nodes, :mreal] = m2p_ref[at : at + nodes, :]
            p2l_pad[d, :, h * LANES : h * LANES + nodes] = p2l_ref[:, at : at + nodes]
            shift_pad[d, :slots, h * LANES : h * LANES + nodes] = shifts_ref[d, :, h * nodes : (h + 1) * nodes]
        lists = lists_ref[d]
        far = lists - (cap + NSIB * 4)
        near = lists - cap
        far_at = lax.shift_right_arithmetic(far, 7) * 64 + (far & 63)
        upper = (far & 64) != 0
        own_at = jnp.where(lists < cap, lists, cap + lax.shift_right_arithmetic(near, 2) * 8 + (near & 3))
        none = jnp.full_like(lists, -1)
        for tile, place in enumerate((
            jnp.where(far < 0, jnp.where(lists < 0, none, own_at), none),
            jnp.where((far >= 0) & jnp.logical_not(upper), far_at, none),
            jnp.where((far >= 0) & upper, far_at, none),
        )):
            place = jnp.concatenate([place, jnp.full((40 - slots, cap), -1, I32)], axis=0)
            rel[tile, d, :, :40] = place.astype(F32).T.astype(BF16)

    def wait_all(ref, sem):
        pltpu.make_async_copy(ref, ref, sem).wait()

    def convert(rows):
        def one(d, c):
            made = lax.dot_general(rows, m2p_pad[d], (((1,), (1,)), ((), ())), preferred_element_type=F32)
            planes[d] = made.astype(BF16)
            return c

        lax.fori_loop(0, dirs, one, 0)

    def step(q, c):
        tile, d = q // dirs, lax.rem(q, dirs)

        def at(cond, when, action):
            @pl.when(cond & (q == when))
            def _():
                action()

        def first_to_second():
            pl.semaphore_wait(in1_sem, 16)
            signal(go1_sem, g + 4)
            serve(4, 4)

        def first_to_third():
            pl.semaphore_wait(in2_sem, 32)
            for ahead in (4, 8, 12):
                signal(go2_sem, g + ahead)
            serve(8, 8)

        def second_to_second():
            pl.semaphore_wait(go1_sem, 1)
            serve(4, 4)

        def second_to_third():
            pl.semaphore_wait(go2_sem, 1)
            serve(8, 8)

        def third_to_rest():
            pl.semaphore_wait(go2_sem, 1)
            serve(4, 4)
            serve(8, 8)

        at(first, SERVE[0][0], first_to_second)
        at(first, SERVE[0][1], first_to_third)
        at(second, SERVE[1][0], second_to_second)
        at(second, SERVE[1][1], second_to_third)
        at(third, SERVE[2][0], third_to_rest)

        @pl.when(q == 0)
        def _():
            wait_all(sib_recv.at[pl.ds(0, 7)], sib_sem)
            own_x[cap : cap + 64] = sib_recv[...].reshape(64, WIDE)
            convert(own_x[...])

        def far_tile(when, which, mine):
            @pl.when((q == when) & mine)
            def _():
                wait_all(recv.at[which, pl.ds(0, 31)], tile_sem.at[which])

            @pl.when((q == when) & jnp.logical_not(mine))
            def _():
                wait_all(recv.at[which], tile_sem.at[which])

            @pl.when(q == when)
            def _():
                convert(recv[which].reshape(TILE, WIDE))

        far_tile(dirs, 0, low)
        far_tile(2 * dirs, 1, third)

        sources = lax.broadcasted_iota(I32, (cap, TILE), 1).astype(F32).astype(BF16)
        table = planes[d]
        real = acc[d, :, :LANES]
        imaginary = acc[d, :, LANES:]
        for j0 in range(0, slots, STACK):
            hot = jnp.concatenate(
                [jnp.where(sources == rel[tile, d, :, j : j + 1], BF16(1), BF16(0)) for j in range(j0, j0 + STACK)],
                axis=0,
            )
            picked = jnp.dot(hot, table, preferred_element_type=F32)
            for n in range(STACK):
                j = j0 + n
                sr, si = shift_pad[d, j : j + 1, :LANES], shift_pad[d, j : j + 1, LANES:]
                pr, pi = picked[n * cap : (n + 1) * cap, :LANES], picked[n * cap : (n + 1) * cap, LANES:]
                real = real + sr * pr - si * pi
                imaginary = imaginary + sr * pi + si * pr
        acc[d, :, :LANES] = real
        acc[d, :, LANES:] = imaginary
        return c

    lax.fori_loop(0, 3 * dirs, step, 0)

    total = jnp.zeros((mreal, cap), F32)
    for d in range(dirs):
        total = total + lax.dot_general(
            p2l_pad[d], acc[d].astype(BF16), (((1,), (1,)), ((), ())), preferred_element_type=F32
        )
    live = lax.broadcasted_iota(I32, (mreal, cap), 1) < count_ref[0]
    out_ref[...] = jnp.where(live, total, F32(0)).astype(BF16)

    wait_all(send.at[pl.ds(0, NY * NZ - 1)], send_sem)
    wait_all(sib_recv.at[pl.ds(0, 7)], sib_send_sem)


def per_device(mult, lists, ghost, sibx, counts, m2p, shifts, p2l):
    mreal, cap = mult.shape
    dirs = lists.shape[0]
    vmem = pl.BlockSpec(memory_space=pltpu.VMEM)
    return pl.pallas_call(
        kernel,
        out_shape=jax.ShapeDtypeStruct((mreal, cap), BF16),
        in_specs=[vmem] * 4 + [pl.BlockSpec(memory_space=pltpu.SMEM)] + [vmem] * 3,
        out_specs=vmem,
        scratch_shapes=[
            pltpu.VMEM((WIDE, cap), BF16),
            pltpu.VMEM((dirs, TILE, WIDE), BF16),
            pltpu.VMEM((dirs, mreal, TILE), BF16),
            pltpu.VMEM((dirs, 40, TILE), F32),
            pltpu.VMEM((3, dirs, cap, LANES), BF16),
            pltpu.VMEM((NY * NZ, 8, WIDE), BF16),
            pltpu.VMEM((8, WIDE), BF16),
            pltpu.VMEM((TILE, WIDE), BF16),
            pltpu.VMEM((NSIB, 8, WIDE), BF16),
            pltpu.VMEM((2, 32, 8, WIDE), BF16),
            pltpu.VMEM((dirs, TILE, TILE), BF16),
            pltpu.VMEM((dirs, cap, TILE), F32),
            pltpu.SemaphoreType.DMA,
            pltpu.SemaphoreType.DMA,
            pltpu.SemaphoreType.DMA,
            pltpu.SemaphoreType.DMA((2,)),
            pltpu.SemaphoreType.REGULAR,
            pltpu.SemaphoreType.REGULAR,
            pltpu.SemaphoreType.REGULAR,
            pltpu.SemaphoreType.REGULAR,
        ],
        compiler_params=pltpu.CompilerParams(
            collective_id=0, has_side_effects=True, vmem_limit_bytes=40 * 2**20
        ),
        cost_estimate=pl.CostEstimate(flops=12 * 10**9, bytes_accessed=3 * 10**6, transcendentals=0),
    )(mult, lists, ghost, sibx, counts, m2p, shifts, p2l)


def solution(mesh):
    both = ("group", "ingroup")
    return jax.shard_map(
        per_device,
        mesh=mesh,
        in_specs=(P(None, both), P(None, None, both), P(both, None), P(both, None), P(both), P(), P(), P()),
        out_specs=P(None, both),
        check_vma=False,
    )
```

time: 419 us -> 69.7 us (0.17)
  the two profiles are of different devices: /device:TPU:8 before, /device:TPU:452 now
where the time goes in v1:
time: 69.7 us; the launch traced here: 69.6 us
  Pallas kernels  65.9 us (95%)
  local copies, waits for them, and re-layouts  2.97 us (4%)
  between operations  0.76 us (1%)
    pallas_call x1, Pallas kernels, per_device(): pl.pallas_call(kernel, out_shape=jax.ShapeDtypeStruct((mreal, cap), BF16)...  65.9 us
    unnamed x14, local copies, waits for them, and re-layouts  2.97 us

profile of v1, /device:TPU:452, one launch (start us, length us, event | category | flops | bytes accessed | tf_op | source)
XLA Modules:
  0.0 69.6 jit_solution(13017014537810750962)
XLA Ops:
  0.7 0.0 copy-start
  0.7 0.0 copy-start.1
  0.7 0.0 copy-start.2
  0.7 0.0 copy-start.3
  0.7 0.0 copy-start.4
  0.7 0.0 copy-start.5
  0.7 2.3 %copy.9.m2p_ref = bf16[1440,338]{1,0:T(8,128)(2,1)S(1)} copy(bf16[1440,338]{0,1:T(8,128)(2,1)} %param.13) | data formatting | bytes 1946880 | tf_op args[5]
  3.0 0.0 copy-done
  3.0 0.0 copy-done.1
  3.0 0.0 copy-done.2
  3.1 0.0 copy-done.3
  3.1 0.0 copy-done.4
  3.1 0.0 copy-done.5
  3.1 65.9 %shard_map.82 = bf16[338,128]{1,0:T(8,128)(2,1)S(1)} custom-call(bf16[338,128]{1,0:T(8,128)(2,1)S(1)} %copy-done.3, s32[6,36,128]{2,1,0:T(8,128)S(1)} %copy-done.2, s32[1,512]{1,0:T(1,128)S(1)} %copy-done.4, s32[1,4]{1,0:T(1,128)S(1)} %copy-done.5, s32[1]{0:T(128)S(6)} %copy.11.count_ref, bf16[1440,338]{1,0:T(8,128)(2,1)S(1)} %copy.9.m2p_ref, ...), custom_call_target="tpu_custom_call" | custom-call | flops 12000000000 | bytes 3000000 | tf_op jit(solution)/shard_map/pallas_call | solution.py:283
  69.0 0.6 copy.12
Async XLA Ops:
  0.7 2.4 %copy-start = (bf16[338,1440]{1,0:T(8,128)(2,1)S(1)}, bf16[338,1440]{1,0:T(8,128)(2,1)}, u32[]{:S(2)}) copy-start(bf16[338,1440]{1,0:T(8,128)(2,1)} %p2l_ref.1) | copy-start | bytes 2920324
  0.7 2.4 %copy-start.1 = (f32[6,36,240]{2,1,0:T(8,128)S(1)}, f32[6,36,240]{2,1,0:T(8,128)}, u32[]{:S(2)}) copy-start(f32[6,36,240]{2,1,0:T(8,128)} %shifts_ref.1) | copy-start | bytes 622084
  0.7 2.4 %copy-start.2 = (s32[6,36,128]{2,1,0:T(8,128)S(1)}, s32[6,36,128]{2,1,0:T(8,128)}, u32[]{:S(2)}) copy-start(s32[6,36,128]{2,1,0:T(8,128)} %lists_ref.1) | copy-start | bytes 331780
  0.7 2.4 %copy-start.3 = (bf16[338,128]{1,0:T(8,128)(2,1)S(1)}, bf16[338,128]{1,0:T(8,128)(2,1)}, u32[]{:S(2)}) copy-start(bf16[338,128]{1,0:T(8,128)(2,1)} %mult_ref.1) | copy-start | bytes 259588
  0.7 2.4 %copy-start.4 = (s32[1,512]{1,0:T(1,128)S(1)}, s32[1,512]{1,0:T(1,128)}, u32[]{:S(2)}) copy-start(s32[1,512]{1,0:T(1,128)} %ghost_ref.1) | copy-start | bytes 6148
  0.7 2.4 %copy-start.5 = (s32[1,4]{1,0:T(1,128)S(1)}, s32[1,4]{1,0:T(1,128)}, u32[]{:S(2)}) copy-start(s32[1,4]{1,0:T(1,128)} %sibx_ref.1) | copy-start | bytes 52

commit v2 on v0

v2 whole, which is shorter than its diff:
```python
import functools

import jax
import jax.numpy as jnp
from jax import lax
from jax.experimental import pallas as pl
from jax.experimental.pallas import tpu as pltpu
from jax.sharding import PartitionSpec as P

MESH = pl.DeviceIdType.MESH
BF16, F32, I32 = jnp.bfloat16, jnp.float32, jnp.int32

LANES = 128
TILE = 256
NY, NZ = 4, 16
NSIB = 8
STACK = 2
WIDE = 384
HALF = 8


def columns_of(row, count):
    wide = jnp.broadcast_to(row.astype(F32), (LANES, count))
    return jnp.concatenate([wide[:, c : c + LANES].T for c in range(0, count, LANES)], axis=0)


def kernel(
    mult_hbm, ghost_hbm, sibx_hbm, count_hbm, lists_hbm, m2p_hbm, shifts_hbm, p2l_hbm, out_ref,
    mult_ref, ghost_ref, sibx_ref, count_ref, lists_ref, m2p_ref, shifts_ref, p2l_ref,
    mult_pad, m2p_pad, p2l_pad, shift_pad, place_cols, places, send, sib_send, rows, sib_recv, recv, planes, acc,
    send_sem, sib_send_sem, sib_sem, tile_sem, load_sem,
):
    g = lax.axis_index("group")
    i = lax.axis_index("ingroup")
    y, z = g // NZ, lax.rem(g, NZ)
    low = z < HALF
    side = z // HALF
    slot = y * HALF + lax.rem(z, HALF)
    dirs, slots = lists_ref.shape[0], lists_ref.shape[1]
    mreal, cap = mult_ref.shape
    nodes = shifts_ref.shape[2] // 2

    barrier = pltpu.get_barrier_semaphore()

    loads = [
        pltpu.make_async_copy(src, dst, load_sem.at[n])
        for n, (src, dst) in enumerate((
            (ghost_hbm, ghost_ref), (mult_hbm, mult_ref), (sibx_hbm, sibx_ref), (count_hbm, count_ref),
            (lists_hbm, lists_ref), (m2p_hbm, m2p_ref), (shifts_hbm, shifts_ref), (p2l_hbm, p2l_ref),
        ))
    ]
    for load in loads:
        load.start()

    def greet_slab(n, c):
        slab = ((y + n) & (NY - 1)) * NZ + ((z + n // NY) & (NZ - 1))
        pl.semaphore_signal(barrier, 1, device_id=(slab, i), device_id_type=MESH)
        return c

    def greet_sibling(n, c):
        pl.semaphore_signal(barrier, 1, device_id=(g, (i + n) & (NSIB - 1)), device_id_type=MESH)
        return c

    lax.fori_loop(1, NY * NZ, greet_slab, 0)
    lax.fori_loop(1, NSIB, greet_sibling, 0)

    mult_pad[...] = jnp.zeros_like(mult_pad)
    for load in loads[:4]:
        load.wait()
    mult_pad[:mreal, :] = mult_ref[...]

    def pick(cols):
        lanes = lax.broadcasted_iota(I32, cols.shape, 1).astype(F32)
        hot = jnp.where(cols == lanes, F32(1), F32(0)).astype(BF16)
        made = lax.dot_general(hot, mult_pad[...], (((1,), (1,)), ((), ())), preferred_element_type=F32)
        return made.astype(BF16)

    n_ghost = ghost_ref.shape[1]
    send[...] = pick(columns_of(ghost_ref[...], n_ghost)).reshape(send.shape)
    sib_row = jnp.concatenate([sibx_ref[...], jnp.full((1, LANES - sibx_ref.shape[1]), -1, I32)], axis=1)
    sib_send[...] = pick(columns_of(sib_row, LANES)[: sib_send.shape[0]])
    sib_recv[i] = sib_send[...]
    recv[side, slot] = send[g]

    lower = lax.broadcasted_iota(I32, (cap, LANES), 1).astype(F32)
    upper = (lower + LANES).astype(BF16)
    lower = lower.astype(BF16)

    def hot_rows(tile, d, j):
        place = places[tile, d, j]
        halves = [jnp.where(lanes == place, BF16(1), BF16(0)) for lanes in (lower, upper)]
        return jnp.concatenate(halves, axis=1)

    def prepare():
        rows[...] = jnp.zeros_like(rows)
        rows[:cap] = pick(lax.broadcasted_iota(I32, (LANES, LANES), 0).astype(F32))
        m2p_pad[...] = jnp.zeros_like(m2p_pad)
        p2l_pad[...] = jnp.zeros_like(p2l_pad)
        shift_pad[...] = jnp.zeros_like(shift_pad)
        acc[...] = jnp.zeros_like(acc)
        for load in loads[4:]:
            load.wait()
        for d in range(dirs):
            for h in range(2):
                at = (2 * d + h) * nodes
                m2p_pad[d, :mreal, h * LANES : h * LANES + nodes] = m2p_ref[:, at : at + nodes]
                p2l_pad[d, :, h * LANES : h * LANES + nodes] = p2l_ref[:, at : at + nodes]
                shift_pad[d, :slots, h * LANES : h * LANES + nodes] = shifts_ref[d, :, h * nodes : (h + 1) * nodes]
            lists = lists_ref[d]
            far = lists - (cap + NSIB * 4)
            near = lists - cap
            far_at = lax.shift_right_arithmetic(far, 7) * 64 + (far & 63)
            far_side = lax.shift_right_arithmetic(far, 6) & 1
            own_at = jnp.where(lists < cap, lists, cap + lax.shift_right_arithmetic(near, 2) * 8 + (near & 3))
            far_at = far_at + jnp.where(far_side == side, TILE, 2 * TILE)
            place = jnp.where(far < 0, own_at, far_at)
            place = jnp.concatenate([place, jnp.full((40 - slots, cap), -1, I32)], axis=0)
            place_cols[d] = place.astype(F32).T

        def spread(d, c):
            for j in range(slots):
                place = jnp.broadcast_to(place_cols[d, :, j : j + 1], (cap, LANES))
                for tile in range(3):
                    places[tile, d, j] = (place - F32(tile * TILE)).astype(BF16)
            return c

        lax.fori_loop(0, dirs, spread, 0)

    def send_all():
        pl.semaphore_wait(barrier, NY * NZ - 1 + NSIB - 1)

        def send_sib(n, c):
            pltpu.make_async_remote_copy(
                src_ref=sib_send,
                dst_ref=sib_recv.at[i],
                send_sem=sib_send_sem,
                recv_sem=sib_sem,
                device_id=(g, (i + n) & (NSIB - 1)),
                device_id_type=MESH,
            ).start()
            return c

        lax.fori_loop(1, NSIB, send_sib, 0)

        def send_slab(n, c):
            to_z = (n // (NY * HALF)) * HALF + ((n // NY + z) & (HALF - 1))
            slab = ((y + n) & (NY - 1)) * NZ + to_z

            @pl.when(slab != g)
            def _():
                pltpu.make_async_remote_copy(
                    src_ref=send.at[slab],
                    dst_ref=recv.at[side, slot],
                    send_sem=send_sem,
                    recv_sem=tile_sem.at[jnp.where(to_z // HALF == side, 0, 1)],
                    device_id=(slab, i),
                    device_id_type=MESH,
                ).start()

            return c

        lax.fori_loop(0, NY * NZ, send_slab, 0)

    def turn(n, c):
        @pl.when((n == 0) == low)
        def _():
            prepare()

        @pl.when((n == 0) != low)
        def _():
            send_all()

        return c

    lax.fori_loop(0, 2, turn, 0)

    def wait_all(ref, sem):
        pltpu.make_async_copy(ref, ref, sem).wait()

    def convert():
        for d in range(dirs):
            planes[d] = jnp.dot(rows[...], m2p_pad[d], preferred_element_type=F32).astype(BF16)

    def add_shifted(tile, d):
        table = planes[d]
        real = acc[d, :, :LANES]
        imaginary = acc[d, :, LANES:]
        for j0 in range(0, slots, STACK):
            hot = jnp.concatenate([hot_rows(tile, d, j) for j in range(j0, j0 + STACK)], axis=0)
            picked = jnp.dot(hot, table, preferred_element_type=F32)
            for n in range(STACK):
                j = j0 + n
                sr, si = shift_pad[d, j : j + 1, :LANES], shift_pad[d, j : j + 1, LANES:]
                pr, pi = picked[n * cap : (n + 1) * cap, :LANES], picked[n * cap : (n + 1) * cap, LANES:]
                real = real + sr * pr - si * pi
                imaginary = imaginary + sr * pi + si * pr
        acc[d, :, :LANES] = real
        acc[d, :, LANES:] = imaginary

    def step(q, c):
        tile, d = q // dirs, lax.rem(q, dirs)

        @pl.when(q == 0)
        def _():
            wait_all(sib_recv.at[pl.ds(0, NSIB - 1)], sib_sem)
            rows[cap : cap + 64] = sib_recv[...].reshape(64, WIDE)

        @pl.when(q == dirs)
        def _():
            wait_all(recv.at[0, pl.ds(0, 31)], tile_sem.at[0])
            rows[...] = recv[side].reshape(TILE, WIDE)

        @pl.when(q == 2 * dirs)
        def _():
            wait_all(recv.at[0], tile_sem.at[1])
            rows[...] = recv[1 - side].reshape(TILE, WIDE)

        @pl.when(d == 0)
        def _():
            convert()

        add_shifted(tile, d)
        return c

    lax.fori_loop(0, 3 * dirs, step, 0)

    total = jnp.zeros((mreal, cap), F32)
    for d in range(dirs):
        total = total + lax.dot_general(
            p2l_pad[d], acc[d].astype(BF16), (((1,), (1,)), ((), ())), preferred_element_type=F32
        )
    live = lax.broadcasted_iota(I32, (mreal, cap), 1) < count_ref[...]
    out_ref[...] = jnp.where(live, total, F32(0)).astype(BF16)

    wait_all(send.at[pl.ds(0, NY * NZ - 1)], send_sem)
    wait_all(sib_recv.at[pl.ds(0, NSIB - 1)], sib_send_sem)


def per_device(mult, lists, ghost, sibx, counts, m2p, shifts, p2l):
    mreal, cap = mult.shape
    dirs = lists.shape[0]
    width = m2p.shape[0]
    hbm = pl.BlockSpec(memory_space=pltpu.HBM)
    return pl.pallas_call(
        kernel,
        out_shape=jax.ShapeDtypeStruct((mreal, cap), BF16),
        in_specs=[hbm] * 8,
        out_specs=pl.BlockSpec(memory_space=pltpu.VMEM),
        scratch_shapes=[
            pltpu.VMEM((mreal, cap), BF16),
            pltpu.VMEM(ghost.shape, I32),
            pltpu.VMEM(sibx.shape, I32),
            pltpu.VMEM((1, 1), I32),
            pltpu.VMEM(lists.shape, I32),
            pltpu.VMEM((mreal, width), BF16),
            pltpu.VMEM(shifts.shape, F32),
            pltpu.VMEM((mreal, width), BF16),
            pltpu.VMEM((WIDE, cap), BF16),
            pltpu.VMEM((dirs, WIDE, TILE), BF16),
            pltpu.VMEM((dirs, mreal, TILE), BF16),
            pltpu.VMEM((dirs, 40, TILE), F32),
            pltpu.VMEM((dirs, cap, 40), F32),
            pltpu.VMEM((3, dirs, lists.shape[1], cap, LANES), BF16),
            pltpu.VMEM((NY * NZ, 8, WIDE), BF16),
            pltpu.VMEM((8, WIDE), BF16),
            pltpu.VMEM((TILE, WIDE), BF16),
            pltpu.VMEM((NSIB, 8, WIDE), BF16),
            pltpu.VMEM((2, NY * HALF, 8, WIDE), BF16),
            pltpu.VMEM((dirs, TILE, TILE), BF16),
            pltpu.VMEM((dirs, cap, TILE), F32),
            pltpu.SemaphoreType.DMA,
            pltpu.SemaphoreType.DMA,
            pltpu.SemaphoreType.DMA,
            pltpu.SemaphoreType.DMA((2,)),
            pltpu.SemaphoreType.DMA((8,)),
        ],
        compiler_params=pltpu.CompilerParams(
            collective_id=0, has_side_effects=True, vmem_limit_bytes=48 * 2**20
        ),
        cost_estimate=pl.CostEstimate(flops=12 * 10**9, bytes_accessed=3 * 10**6, transcendentals=0),
    )(mult, ghost, sibx, counts.reshape(1, 1), lists, m2p.T, shifts, p2l)


def solution(mesh):
    both = ("group", "ingroup")
    return jax.shard_map(
        per_device,
        mesh=mesh,
        in_specs=(P(None, both), P(None, None, both), P(both, None), P(both, None), P(both), P(), P(), P()),
        out_specs=P(None, both),
        check_vma=False,
    )
```

time: 419 us -> 56.1 us (0.13)
  the two profiles are of different devices: /device:TPU:8 before, /device:TPU:34 now
where the time goes in v2:
time: 56.1 us; the launch traced here: 55.8 us
  Pallas kernels  48 us (86%)
  local copies, waits for them, and re-layouts  7.16 us (13%)
  between operations  0.67 us (1%)
    pallas_call x1, Pallas kernels, per_device(): pl.pallas_call(kernel, out_shape=jax.ShapeDtypeStruct((mreal, cap), BF16)...  48 us
    unnamed x15, local copies, waits for them, and re-layouts  7.16 us

profile of v2, /device:TPU:34, one launch (start us, length us, event | category | flops | bytes accessed | tf_op | source)
XLA Modules:
  0.0 55.8 jit_solution(6652067027503982098)
XLA Ops:
  0.7 0.0 copy-start
  0.7 1.2 %copy-done = bf16[1440,338]{0,1:T(8,128)(2,1)S(1)} copy-done((bf16[1440,338]{0,1:T(8,128)(2,1)S(1)}, bf16[1440,338]{0,1:T(8,128)(2,1)}, u32[]{:S(2)}) %copy-start) | copy-done | bytes 973464
  1.9 0.0 copy-start.1
  1.9 1.2 %copy-done.1 = bf16[338,1440]{1,0:T(8,128)(2,1)S(1)} copy-done((bf16[338,1440]{1,0:T(8,128)(2,1)S(1)}, bf16[338,1440]{1,0:T(8,128)(2,1)}, u32[]{:S(2)}) %copy-start.1) | copy-done | bytes 973464
  3.1 0.0 copy-start.2
  3.1 0.9 %copy-done.2 = f32[6,36,240]{2,1,0:T(8,128)S(1)} copy-done((f32[6,36,240]{2,1,0:T(8,128)S(1)}, f32[6,36,240]{2,1,0:T(8,128)}, u32[]{:S(2)}) %copy-start.2) | copy-done | bytes 207384
  4.1 0.0 copy-start.3
  4.1 0.9 %copy-done.3 = s32[6,36,128]{2,1,0:T(8,128)S(1)} copy-done((s32[6,36,128]{2,1,0:T(8,128)S(1)}, s32[6,36,128]{2,1,0:T(8,128)}, u32[]{:S(2)}) %copy-start.3) | copy-done | bytes 110616
  5.0 0.0 copy-start.4
  5.0 0.9 %copy-done.4 = bf16[338,128]{1,0:T(8,128)(2,1)S(1)} copy-done((bf16[338,128]{1,0:T(8,128)(2,1)S(1)}, bf16[338,128]{1,0:T(8,128)(2,1)}, u32[]{:S(2)}) %copy-start.4) | copy-done | bytes 86552
  5.8 0.0 copy-start.5
  5.8 0.7 %copy-done.5 = s32[1,512]{1,0:T(1,128)S(1)} copy-done((s32[1,512]{1,0:T(1,128)S(1)}, s32[1,512]{1,0:T(1,128)}, u32[]{:S(2)}) %copy-start.5) | copy-done | bytes 2072
  6.5 0.0 copy-start.6
  6.5 0.7 %copy-done.6 = s32[1,4]{1,0:T(1,128)S(1)} copy-done((s32[1,4]{1,0:T(1,128)S(1)}, s32[1,4]{1,0:T(1,128)}, u32[]{:S(2)}) %copy-start.6) | copy-done | bytes 40
  7.2 48.0 %shard_map.82 = bf16[338,128]{1,0:T(8,128)(2,1)S(1)} custom-call(bf16[338,128]{1,0:T(8,128)(2,1)S(1)} %copy-done.4, s32[1,512]{1,0:T(1,128)S(1)} %copy-done.5, s32[1,4]{1,0:T(1,128)S(1)} %copy-done.6, s32[1,1]{1,0:T(1,128)} %bitcast.2.count_hbm, s32[6,36,128]{2,1,0:T(8,128)S(1)} %copy-done.3, bf16[338,1440]{1,0:T(8,128)(2,1)S(1)} %bitcast.3, ...), custom_call_target="tpu_custom_call" | custom-call | flops 12000000000 | bytes 3000000 | tf_op jit(solution)/shard_map/pallas_call | solution.py:244
  55.2 0.6 %copy.11 = bf16[338,128]{1,0:T(8,128)(2,1)} copy(bf16[338,128]{1,0:T(8,128)(2,1)S(1)} %shard_map.82) | data formatting | bytes 173056
Async XLA Ops:
  0.7 1.2 %copy-start = (bf16[1440,338]{0,1:T(8,128)(2,1)S(1)}, bf16[1440,338]{0,1:T(8,128)(2,1)}, u32[]{:S(2)}) copy-start(bf16[1440,338]{0,1:T(8,128)(2,1)} %param.13) | copy-start | bytes 2920324
  1.9 1.2 %copy-start.1 = (bf16[338,1440]{1,0:T(8,128)(2,1)S(1)}, bf16[338,1440]{1,0:T(8,128)(2,1)}, u32[]{:S(2)}) copy-start(bf16[338,1440]{1,0:T(8,128)(2,1)} %p2l_hbm.1) | copy-start | bytes 2920324
  3.1 0.9 %copy-start.2 = (f32[6,36,240]{2,1,0:T(8,128)S(1)}, f32[6,36,240]{2,1,0:T(8,128)}, u32[]{:S(2)}) copy-start(f32[6,36,240]{2,1,0:T(8,128)} %shifts_hbm.1) | copy-start | bytes 622084
  4.1 0.9 %copy-start.3 = (s32[6,36,128]{2,1,0:T(8,128)S(1)}, s32[6,36,128]{2,1,0:T(8,128)}, u32[]{:S(2)}) copy-start(s32[6,36,128]{2,1,0:T(8,128)} %lists_hbm.1) | copy-start | bytes 331780
  5.0 0.9 %copy-start.4 = (bf16[338,128]{1,0:T(8,128)(2,1)S(1)}, bf16[338,128]{1,0:T(8,128)(2,1)}, u32[]{:S(2)}) copy-start(bf16[338,128]{1,0:T(8,128)(2,1)} %mult_hbm.1) | copy-start | bytes 259588
  5.8 0.7 %copy-start.5 = (s32[1,512]{1,0:T(1,128)S(1)}, s32[1,512]{1,0:T(1,128)}, u32[]{:S(2)}) copy-start(s32[1,512]{1,0:T(1,128)} %ghost_hbm.1) | copy-start | bytes 6148
  6.5 0.7 %copy-start.6 = (s32[1,4]{1,0:T(1,128)S(1)}, s32[1,4]{1,0:T(1,128)}, u32[]{:S(2)}) copy-start(s32[1,4]{1,0:T(1,128)} %sibx_hbm.1) | copy-start | bytes 52

commit v3 on v2

--- a/solution.py
+++ b/solution.py
@@ -86,9 +86,10 @@
     upper = (lower + LANES).astype(BF16)
     lower = lower.astype(BF16)
 
-    def hot_rows(tile, d, j):
-        place = places[tile, d, j]
-        halves = [jnp.where(lanes == place, BF16(1), BF16(0)) for lanes in (lower, upper)]
+    def hot_rows(tiles, d, j):
+        halves = [
+            jnp.where(lanes == places[tile, d, j], BF16(1), BF16(0)) for tile in tiles for lanes in (lower, upper)
+        ]
         return jnp.concatenate(halves, axis=1)
 
     def prepare():
@@ -177,16 +178,17 @@
     def wait_all(ref, sem):
         pltpu.make_async_copy(ref, ref, sem).wait()
 
-    def convert():
+    def convert(first):
         for d in range(dirs):
-            planes[d] = jnp.dot(rows[...], m2p_pad[d], preferred_element_type=F32).astype(BF16)
-
-    def add_shifted(tile, d):
-        table = planes[d]
+            made = jnp.dot(rows[...], m2p_pad[d], preferred_element_type=F32)
+            planes[d, first : first + TILE] = made.astype(BF16)
+
+    def add_shifted(tiles, d):
+        table = planes[d, : len(tiles) * TILE]
         real = acc[d, :, :LANES]
         imaginary = acc[d, :, LANES:]
         for j0 in range(0, slots, STACK):
-            hot = jnp.concatenate([hot_rows(tile, d, j) for j in range(j0, j0 + STACK)], axis=0)
+            hot = jnp.concatenate([hot_rows(tiles, d, j) for j in range(j0, j0 + STACK)], axis=0)
             picked = jnp.dot(hot, table, preferred_element_type=F32)
             for n in range(STACK):
                 j = j0 + n
@@ -197,32 +199,28 @@
         acc[d, :, :LANES] = real
         acc[d, :, LANES:] = imaginary
 
-    def step(q, c):
-        tile, d = q // dirs, lax.rem(q, dirs)
-
-        @pl.when(q == 0)
-        def _():
-            wait_all(sib_recv.at[pl.ds(0, NSIB - 1)], sib_sem)
-            rows[cap : cap + 64] = sib_recv[...].reshape(64, WIDE)
-
-        @pl.when(q == dirs)
-        def _():
-            wait_all(recv.at[0, pl.ds(0, 31)], tile_sem.at[0])
-            rows[...] = recv[side].reshape(TILE, WIDE)
-
-        @pl.when(q == 2 * dirs)
-        def _():
-            wait_all(recv.at[0], tile_sem.at[1])
-            rows[...] = recv[1 - side].reshape(TILE, WIDE)
-
-        @pl.when(d == 0)
-        def _():
-            convert()
-
-        add_shifted(tile, d)
-        return c
-
-    lax.fori_loop(0, 3 * dirs, step, 0)
+    wait_all(sib_recv.at[pl.ds(0, NSIB - 1)], sib_sem)
+    rows[cap : cap + 64] = sib_recv[...].reshape(64, WIDE)
+    convert(0)
+
+    def home_step(d, c):
+        add_shifted((0,), d)
+        return c
+
+    lax.fori_loop(0, dirs, home_step, 0)
+
+    wait_all(recv.at[0, pl.ds(0, 31)], tile_sem.at[0])
+    rows[...] = recv[side].reshape(TILE, WIDE)
+    convert(0)
+    wait_all(recv.at[0], tile_sem.at[1])
+    rows[...] = recv[1 - side].reshape(TILE, WIDE)
+    convert(TILE)
+
+    def slab_step(d, c):
+        add_shifted((1, 2), d)
+        return c
+
+    lax.fori_loop(0, dirs, slab_step, 0)
 
     total = jnp.zeros((mreal, cap), F32)
     for d in range(dirs):
@@ -266,7 +264,7 @@
             pltpu.VMEM((TILE, WIDE), BF16),
             pltpu.VMEM((NSIB, 8, WIDE), BF16),
             pltpu.VMEM((2, NY * HALF, 8, WIDE), BF16),
-            pltpu.VMEM((dirs, TILE, TILE), BF16),
+            pltpu.VMEM((dirs, 2 * TILE, TILE), BF16),
             pltpu.VMEM((dirs, cap, TILE), F32),
             pltpu.SemaphoreType.DMA,
             pltpu.SemaphoreType.DMA,

time: 56.1 us -> 52.7 us (0.939)
  the two profiles are of different devices: /device:TPU:34 before, /device:TPU:192 now
where the time goes in v3:
time: 52.7 us; the launch traced here: 52.4 us
  Pallas kernels  44.6 us (85%)
  local copies, waits for them, and re-layouts  7.16 us (14%)
  between operations  0.67 us (1%)
    pallas_call x1, Pallas kernels, per_device(): pl.pallas_call(kernel, out_shape=jax.ShapeDtypeStruct((mreal, cap), BF16)...  44.6 us
    unnamed x15, local copies, waits for them, and re-layouts  7.16 us

profile of v3, /device:TPU:192, one launch (start us, length us, event | category | flops | bytes accessed | tf_op | source)
XLA Modules:
  0.0 52.4 jit_solution(15682443810040390629)
XLA Ops:
  0.7 0.0 copy-start
  0.7 1.2 %copy-done = bf16[1440,338]{0,1:T(8,128)(2,1)S(1)} copy-done((bf16[1440,338]{0,1:T(8,128)(2,1)S(1)}, bf16[1440,338]{0,1:T(8,128)(2,1)}, u32[]{:S(2)}) %copy-start) | copy-done | bytes 973464
  1.9 0.0 copy-start.1
  1.9 1.2 %copy-done.1 = bf16[338,1440]{1,0:T(8,128)(2,1)S(1)} copy-done((bf16[338,1440]{1,0:T(8,128)(2,1)S(1)}, bf16[338,1440]{1,0:T(8,128)(2,1)}, u32[]{:S(2)}) %copy-start.1) | copy-done | bytes 973464
  3.1 0.0 copy-start.2
  3.1 0.9 %copy-done.2 = f32[6,36,240]{2,1,0:T(8,128)S(1)} copy-done((f32[6,36,240]{2,1,0:T(8,128)S(1)}, f32[6,36,240]{2,1,0:T(8,128)}, u32[]{:S(2)}) %copy-start.2) | copy-done | bytes 207384
  4.1 0.0 copy-start.3
  4.1 0.9 %copy-done.3 = s32[6,36,128]{2,1,0:T(8,128)S(1)} copy-done((s32[6,36,128]{2,1,0:T(8,128)S(1)}, s32[6,36,128]{2,1,0:T(8,128)}, u32[]{:S(2)}) %copy-start.3) | copy-done | bytes 110616
  5.0 0.0 copy-start.4
  5.0 0.9 %copy-done.4 = bf16[338,128]{1,0:T(8,128)(2,1)S(1)} copy-done((bf16[338,128]{1,0:T(8,128)(2,1)S(1)}, bf16[338,128]{1,0:T(8,128)(2,1)}, u32[]{:S(2)}) %copy-start.4) | copy-done | bytes 86552
  5.8 0.0 copy-start.5
  5.8 0.7 %copy-done.5 = s32[1,512]{1,0:T(1,128)S(1)} copy-done((s32[1,512]{1,0:T(1,128)S(1)}, s32[1,512]{1,0:T(1,128)}, u32[]{:S(2)}) %copy-start.5) | copy-done | bytes 2072
  6.5 0.0 copy-start.6
  6.5 0.7 %copy-done.6 = s32[1,4]{1,0:T(1,128)S(1)} copy-done((s32[1,4]{1,0:T(1,128)S(1)}, s32[1,4]{1,0:T(1,128)}, u32[]{:S(2)}) %copy-start.6) | copy-done | bytes 40
  7.2 44.6 %shard_map.82 = bf16[338,128]{1,0:T(8,128)(2,1)S(1)} custom-call(bf16[338,128]{1,0:T(8,128)(2,1)S(1)} %copy-done.4, s32[1,512]{1,0:T(1,128)S(1)} %copy-done.5, s32[1,4]{1,0:T(1,128)S(1)} %copy-done.6, s32[1,1]{1,0:T(1,128)} %bitcast.2.count_hbm, s32[6,36,128]{2,1,0:T(8,128)S(1)} %copy-done.3, bf16[338,1440]{1,0:T(8,128)(2,1)S(1)} %bitcast.3, ...), custom_call_target="tpu_custom_call" | custom-call | flops 12000000000 | bytes 3000000 | tf_op jit(solution)/shard_map/pallas_call | solution.py:242
  51.8 0.6 %copy.11 = bf16[338,128]{1,0:T(8,128)(2,1)} copy(bf16[338,128]{1,0:T(8,128)(2,1)S(1)} %shard_map.82) | data formatting | bytes 173056
Async XLA Ops:
  0.7 1.2 %copy-start = (bf16[1440,338]{0,1:T(8,128)(2,1)S(1)}, bf16[1440,338]{0,1:T(8,128)(2,1)}, u32[]{:S(2)}) copy-start(bf16[1440,338]{0,1:T(8,128)(2,1)} %param.13) | copy-start | bytes 2920324
  1.9 1.2 %copy-start.1 = (bf16[338,1440]{1,0:T(8,128)(2,1)S(1)}, bf16[338,1440]{1,0:T(8,128)(2,1)}, u32[]{:S(2)}) copy-start(bf16[338,1440]{1,0:T(8,128)(2,1)} %p2l_hbm.1) | copy-start | bytes 2920324
  3.1 0.9 %copy-start.2 = (f32[6,36,240]{2,1,0:T(8,128)S(1)}, f32[6,36,240]{2,1,0:T(8,128)}, u32[]{:S(2)}) copy-start(f32[6,36,240]{2,1,0:T(8,128)} %shifts_hbm.1) | copy-start | bytes 622084
  4.1 0.9 %copy-start.3 = (s32[6,36,128]{2,1,0:T(8,128)S(1)}, s32[6,36,128]{2,1,0:T(8,128)}, u32[]{:S(2)}) copy-start(s32[6,36,128]{2,1,0:T(8,128)} %lists_hbm.1) | copy-start | bytes 331780
  5.0 0.9 %copy-start.4 = (bf16[338,128]{1,0:T(8,128)(2,1)S(1)}, bf16[338,128]{1,0:T(8,128)(2,1)}, u32[]{:S(2)}) copy-start(bf16[338,128]{1,0:T(8,128)(2,1)} %mult_hbm.1) | copy-start | bytes 259588
  5.8 0.7 %copy-start.5 = (s32[1,512]{1,0:T(1,128)S(1)}, s32[1,512]{1,0:T(1,128)}, u32[]{:S(2)}) copy-start(s32[1,512]{1,0:T(1,128)} %ghost_hbm.1) | copy-start | bytes 6148
  6.5 0.7 %copy-start.6 = (s32[1,4]{1,0:T(1,128)S(1)}, s32[1,4]{1,0:T(1,128)}, u32[]{:S(2)}) copy-start(s32[1,4]{1,0:T(1,128)} %sibx_hbm.1) | copy-start | bytes 52

commit v4 on v3

--- a/solution.py
+++ b/solution.py
@@ -49,7 +49,7 @@
             (lists_hbm, lists_ref), (m2p_hbm, m2p_ref), (shifts_hbm, shifts_ref), (p2l_hbm, p2l_ref),
         ))
     ]
-    for load in loads:
+    for load in loads[:4]:
         load.start()
 
     def greet_slab(n, c):
@@ -63,6 +63,8 @@
 
     lax.fori_loop(1, NY * NZ, greet_slab, 0)
     lax.fori_loop(1, NSIB, greet_sibling, 0)
+    for load in loads[4:]:
+        load.start()
 
     mult_pad[...] = jnp.zeros_like(mult_pad)
     for load in loads[:4]:
@@ -141,7 +143,6 @@
             ).start()
             return c
 
-        lax.fori_loop(1, NSIB, send_sib, 0)
 
         def send_slab(n, c):
             to_z = (n // (NY * HALF)) * HALF + ((n // NY + z) & (HALF - 1))
@@ -161,6 +162,7 @@
             return c
 
         lax.fori_loop(0, NY * NZ, send_slab, 0)
+        lax.fori_loop(1, NSIB, send_sib, 0)
 
     def turn(n, c):
         @pl.when((n == 0) == low)

time: 52.7 us -> 52.5 us (level)
  the two profiles are of different devices: /device:TPU:192 before, /device:TPU:454 now
where the time goes in v4:
time: 52.5 us; the launch traced here: 52.2 us
  Pallas kernels  44.3 us (84%)
  local copies, waits for them, and re-layouts  7.16 us (14%)
  between operations  0.67 us (1%)
    pallas_call x1, Pallas kernels, per_device(): pl.pallas_call(kernel, out_shape=jax.ShapeDtypeStruct((mreal, cap), BF16)...  44.3 us
    unnamed x15, local copies, waits for them, and re-layouts  7.16 us

profile of v4, /device:TPU:454, one launch (start us, length us, event | category | flops | bytes accessed | tf_op | source)
XLA Modules:
  0.0 52.2 jit_solution(14517228420195301294)
XLA Ops:
  0.7 0.0 copy-start
  0.7 1.2 %copy-done = bf16[1440,338]{0,1:T(8,128)(2,1)S(1)} copy-done((bf16[1440,338]{0,1:T(8,128)(2,1)S(1)}, bf16[1440,338]{0,1:T(8,128)(2,1)}, u32[]{:S(2)}) %copy-start) | copy-done | bytes 973464
  1.9 0.0 copy-start.1
  1.9 1.2 %copy-done.1 = bf16[338,1440]{1,0:T(8,128)(2,1)S(1)} copy-done((bf16[338,1440]{1,0:T(8,128)(2,1)S(1)}, bf16[338,1440]{1,0:T(8,128)(2,1)}, u32[]{:S(2)}) %copy-start.1) | copy-done | bytes 973464
  3.1 0.0 copy-start.2
  3.1 0.9 %copy-done.2 = f32[6,36,240]{2,1,0:T(8,128)S(1)} copy-done((f32[6,36,240]{2,1,0:T(8,128)S(1)}, f32[6,36,240]{2,1,0:T(8,128)}, u32[]{:S(2)}) %copy-start.2) | copy-done | bytes 207384
  4.1 0.0 copy-start.3
  4.1 0.9 %copy-done.3 = s32[6,36,128]{2,1,0:T(8,128)S(1)} copy-done((s32[6,36,128]{2,1,0:T(8,128)S(1)}, s32[6,36,128]{2,1,0:T(8,128)}, u32[]{:S(2)}) %copy-start.3) | copy-done | bytes 110616
  5.0 0.0 copy-start.4
  5.0 0.9 %copy-done.4 = bf16[338,128]{1,0:T(8,128)(2,1)S(1)} copy-done((bf16[338,128]{1,0:T(8,128)(2,1)S(1)}, bf16[338,128]{1,0:T(8,128)(2,1)}, u32[]{:S(2)}) %copy-start.4) | copy-done | bytes 86552
  5.8 0.0 copy-start.5
  5.8 0.7 %copy-done.5 = s32[1,512]{1,0:T(1,128)S(1)} copy-done((s32[1,512]{1,0:T(1,128)S(1)}, s32[1,512]{1,0:T(1,128)}, u32[]{:S(2)}) %copy-start.5) | copy-done | bytes 2072
  6.5 0.0 copy-start.6
  6.5 0.7 %copy-done.6 = s32[1,4]{1,0:T(1,128)S(1)} copy-done((s32[1,4]{1,0:T(1,128)S(1)}, s32[1,4]{1,0:T(1,128)}, u32[]{:S(2)}) %copy-start.6) | copy-done | bytes 40
  7.2 44.3 %shard_map.82 = bf16[338,128]{1,0:T(8,128)(2,1)S(1)} custom-call(bf16[338,128]{1,0:T(8,128)(2,1)S(1)} %copy-done.4, s32[1,512]{1,0:T(1,128)S(1)} %copy-done.5, s32[1,4]{1,0:T(1,128)S(1)} %copy-done.6, s32[1,1]{1,0:T(1,128)} %bitcast.2.count_hbm, s32[6,36,128]{2,1,0:T(8,128)S(1)} %copy-done.3, bf16[338,1440]{1,0:T(8,128)(2,1)S(1)} %bitcast.3, ...), custom_call_target="tpu_custom_call" | custom-call | flops 12000000000 | bytes 3000000 | tf_op jit(solution)/shard_map/pallas_call | solution.py:244
  51.5 0.6 %copy.11 = bf16[338,128]{1,0:T(8,128)(2,1)} copy(bf16[338,128]{1,0:T(8,128)(2,1)S(1)} %shard_map.82) | data formatting | bytes 173056
Async XLA Ops:
  0.7 1.2 %copy-start = (bf16[1440,338]{0,1:T(8,128)(2,1)S(1)}, bf16[1440,338]{0,1:T(8,128)(2,1)}, u32[]{:S(2)}) copy-start(bf16[1440,338]{0,1:T(8,128)(2,1)} %param.13) | copy-start | bytes 2920324
  1.9 1.2 %copy-start.1 = (bf16[338,1440]{1,0:T(8,128)(2,1)S(1)}, bf16[338,1440]{1,0:T(8,128)(2,1)}, u32[]{:S(2)}) copy-start(bf16[338,1440]{1,0:T(8,128)(2,1)} %p2l_hbm.1) | copy-start | bytes 2920324
  3.1 0.9 %copy-start.2 = (f32[6,36,240]{2,1,0:T(8,128)S(1)}, f32[6,36,240]{2,1,0:T(8,128)}, u32[]{:S(2)}) copy-start(f32[6,36,240]{2,1,0:T(8,128)} %shifts_hbm.1) | copy-start | bytes 622084
  4.1 0.9 %copy-start.3 = (s32[6,36,128]{2,1,0:T(8,128)S(1)}, s32[6,36,128]{2,1,0:T(8,128)}, u32[]{:S(2)}) copy-start(s32[6,36,128]{2,1,0:T(8,128)} %lists_hbm.1) | copy-start | bytes 331780
  5.0 0.9 %copy-start.4 = (bf16[338,128]{1,0:T(8,128)(2,1)S(1)}, bf16[338,128]{1,0:T(8,128)(2,1)}, u32[]{:S(2)}) copy-start(bf16[338,128]{1,0:T(8,128)(2,1)} %mult_hbm.1) | copy-start | bytes 259588
  5.8 0.7 %copy-start.5 = (s32[1,512]{1,0:T(1,128)S(1)}, s32[1,512]{1,0:T(1,128)}, u32[]{:S(2)}) copy-start(s32[1,512]{1,0:T(1,128)} %ghost_hbm.1) | copy-start | bytes 6148
  6.5 0.7 %copy-start.6 = (s32[1,4]{1,0:T(1,128)S(1)}, s32[1,4]{1,0:T(1,128)}, u32[]{:S(2)}) copy-start(s32[1,4]{1,0:T(1,128)} %sibx_hbm.1) | copy-start | bytes 52
